TPU v7x, 32 devices: a whole 2x2x4 slice. The times are simulated.
32 devices in a mesh: grp: 4 (over x, core), tile: 8 (over z, y).
Axes of the slice: x: 2, y: 2, z: 4, core: 2. Of those that a mesh axis runs over, the one named last changes fastest.
Arguments:
- height_model: float32 [4608, 1024], P('grp', 'tile'), as said below
- scenario_trigger_indicator: int32 [4, 256, 512], P('grp', 'tile'), may hold values 0 or 1
- initial_snow_thickness_cm: int32 [4, 256, 512], P('grp', 'tile'), may hold values from 20 to 300
- frame_leading_northing_index: int32 [4], P('grp'), may hold values from 3 to 4349
- frame_leading_easting_index: int32 [4], P('grp'), may hold values from 3 to 509
Outputs:
- ground_geometry: float32 [4, 4608, 1024], P(None, 'grp', 'tile')
- flow: float32 [4, 3, 256, 512], P('grp', None, 'tile')
Inputs may be any that keep to these rules, and one draw needn't show every extreme that they name: `frame_leading_northing_index`: each window, widened by 3 cells on every side, lies inside the DEM rows. `frame_leading_easting_index`: each window, widened by 3 cells on every side, lies inside the DEM columns. `height_model`: elevation in metres, near zero at the DEM's rim within a few metres.
All inputs are finite; a program needn't handle non-finite values. No bound on the sum of `scenario_trigger_indicator` on one device may be relied on, other than what follows from the above.
Results may differ from a plain program's by a relative error of at most 0.0003.
Values sent between devices are 32-bit elements; how exact they have to be, the bound alone decides.
A program may use at most 64 MiB of HBM per device.

v0:
```python
import jax
import jax.numpy as jnp
from jax import lax
from jax.sharding import PartitionSpec as P

KERNEL_SPAN = 3
STEPS = 4
cell_size = 2.0
gravity = 9.81
time_step = 0.1
friction = 0.2
turbulence = 500.0
depth_floor = 0.1
speed_floor = 0.5
binomial = (0.0625, 0.25, 0.375, 0.25, 0.0625)


def padded(shard, sides, width):
    for axis, dim in sides:
        size, length = (lax.axis_size(axis), shard.shape[dim])
        up = [(i, (i + 1) % size) for i in range(size - 1)]
        down = [(j, i) for i, j in up]
        last = lax.slice_in_dim(shard, length - width, length, axis=dim)
        leading = lax.slice_in_dim(shard, 0, width, axis=dim)
        before = lax.ppermute(last, axis, up)
        after = lax.ppermute(leading, axis, down)
        shard = jnp.concatenate([before, shard, after], axis=dim)
    return shard


def derive_gradient_fields(framed_elevation_grid):
    inner_rows = framed_elevation_grid.shape[0] - 2 * KERNEL_SPAN
    inner_cols = framed_elevation_grid.shape[1] - 2 * KERNEL_SPAN
    across = binomial[0] * framed_elevation_grid[0 : inner_rows + 2, :]
    for offset in range(1, 5):
        across = (
            across + binomial[offset] * framed_elevation_grid[offset : offset + inner_rows + 2, :]
        )
    smooth = binomial[0] * across[:, 0 : inner_cols + 2]
    for offset in range(1, 5):
        smooth = smooth + binomial[offset] * across[:, offset : offset + inner_cols + 2]
    centre = smooth[1:-1, 1:-1]
    upper_cell = smooth[2:, 1:-1]
    lower_cell = smooth[:-2, 1:-1]
    right_cell = smooth[1:-1, 2:]
    left_cell = smooth[1:-1, :-2]
    grad_rows = (upper_cell - lower_cell) / (2.0 * cell_size)
    grad_cols = (right_cell - left_cell) / (2.0 * cell_size)
    curvature = (upper_cell + lower_cell + right_cell + left_cell - 4.0 * centre) / (
        cell_size * cell_size
    )
    upright = 1.0 / jnp.sqrt(1.0 + grad_rows * grad_rows + grad_cols * grad_cols)
    return jnp.stack([-grad_rows * upright, -grad_cols * upright, upright, curvature])


def advance(framed_elevation_grid, patch):
    depth_now = framed_elevation_grid[0]
    momentum_a = framed_elevation_grid[1]
    momentum_b = framed_elevation_grid[2]
    safe_depth = jnp.maximum(depth_now, depth_floor)
    velocity_a = momentum_a / safe_depth
    velocity_b = momentum_b / safe_depth
    wave_speed = jnp.sqrt(gravity * (jnp.maximum(depth_now, 0.0) + depth_floor))
    pressure = 0.5 * gravity * depth_now * depth_now
    flux_rows = jnp.stack([momentum_a, momentum_a * velocity_a + pressure, momentum_b * velocity_a])
    flux_cols = jnp.stack([momentum_b, momentum_a * velocity_b, momentum_b * velocity_b + pressure])
    reach_rows = jnp.abs(velocity_a) + wave_speed
    reach_cols = jnp.abs(velocity_b) + wave_speed
    bound_rows = jnp.maximum(reach_rows[:-1, 1:-1], reach_rows[1:, 1:-1])
    face_rows = 0.5 * (flux_rows[:, :-1, 1:-1] + flux_rows[:, 1:, 1:-1]) - 0.5 * bound_rows * (
        framed_elevation_grid[:, 1:, 1:-1] - framed_elevation_grid[:, :-1, 1:-1]
    )
    bound_cols = jnp.maximum(reach_cols[1:-1, :-1], reach_cols[1:-1, 1:])
    face_cols = 0.5 * (flux_cols[:, 1:-1, :-1] + flux_cols[:, 1:-1, 1:]) - 0.5 * bound_cols * (
        framed_elevation_grid[:, 1:-1, 1:] - framed_elevation_grid[:, 1:-1, :-1]
    )
    interior = framed_elevation_grid[:, 1:-1, 1:-1]
    updated = interior - time_step / cell_size * (
        face_rows[:, 1:] - face_rows[:, :-1] + face_cols[:, :, 1:] - face_cols[:, :, :-1]
    )
    new_depth = updated[0]
    drive_a = updated[1] + time_step * gravity * interior[0] * patch[0]
    drive_b = updated[2] + time_step * gravity * interior[0] * patch[1]
    floor_depth = jnp.maximum(new_depth, depth_floor)
    rate_a = drive_a / floor_depth
    rate_b = drive_b / floor_depth
    square = rate_a * rate_a + rate_b * rate_b
    speed_norm = jnp.sqrt(square + speed_floor * speed_floor)
    normal_load = jnp.maximum(gravity * patch[2] + patch[3] * square, 0.0)
    drag_factor = time_step * (
        friction * normal_load / speed_norm + gravity * speed_norm / (turbulence * floor_depth)
    )
    return jnp.stack([new_depth, drive_a / (1.0 + drag_factor), drive_b / (1.0 + drag_factor)])


def shards(
    height_model,
    scenario_trigger_indicator,
    initial_snow_thickness_cm,
    frame_leading_northing_index,
    frame_leading_easting_index,
):
    tile_count = lax.axis_size("tile")
    piece_rows = scenario_trigger_indicator.shape[1]
    window_width = scenario_trigger_indicator.shape[2]
    window_height = piece_rows * tile_count
    block_lateral_number = height_model.shape[1]
    framed_elevation_grid = padded(height_model, (("grp", 0), ("tile", 1)), KERNEL_SPAN)
    ground_geometry = derive_gradient_fields(framed_elevation_grid)
    first_row = frame_leading_northing_index[0]
    first_col = frame_leading_easting_index[0]
    column_strip = lax.all_gather(ground_geometry, "grp", axis=1, tiled=True)
    row_band = lax.dynamic_slice_in_dim(column_strip, first_row, window_height, 1)
    blocks = row_band.reshape(4, tile_count, piece_rows, block_lateral_number)
    rows_wide = lax.all_to_all(blocks, "tile", split_axis=1, concat_axis=3, tiled=True)
    rows_wide = rows_wide.reshape(4, piece_rows, tile_count * block_lateral_number)
    under_window = lax.dynamic_slice_in_dim(rows_wide, first_col, window_width, 2)
    release_depth = (
        scenario_trigger_indicator[0].astype(jnp.float32)
        * initial_snow_thickness_cm[0].astype(jnp.float32)
        * 0.01
    )
    empty_field = jnp.zeros_like(release_depth)
    flow_state = jnp.stack([release_depth, empty_field, empty_field])
    for turn_index in range(STEPS):
        extended = padded(flow_state, (("tile", 1),), 1)
        flow_state = advance(jnp.pad(extended, ((0, 0), (0, 0), (1, 1))), under_window)
    return (ground_geometry, flow_state[None])


def solution(mesh):
    return jax.shard_map(
        shards,
        mesh=mesh,
        in_specs=(
            P("grp", "tile"),
            P("grp", "tile", None),
            P("grp", "tile", None),
            P("grp"),
            P("grp"),
        ),
        out_specs=(P(None, "grp", "tile"), P("grp", None, "tile", None)),
        check_vma=False,
    )
```

profile of v0, /device:TPU:16, one launch (start us, length us, event | category | flops | bytes accessed | tf_op | source)
XLA Modules:
  0.0 159.4 jit_solution(9979088048718649279)
XLA Ops:
  7.2 0.7 fusion.58
  7.9 1.7 %collective-permute-start = (f32[3,128]{1,0:T(4,128)S(1)}, f32[3,128]{1,0:T(4,128)S(1)}, u32[]{:S(2)}, u32[]{:S(2)}) collective-permute-start(f32[3,128]{1,0:T(4,128)S(1)} %get-tuple-element.21), channel_id=1, source_target_pairs={{0,8},{8,16},{16,24},{1,9},{9,17},{17,25},{2,10},{10,18},{18,26},{... | collective-permute-start | bytes 4616 | tf_op jit(solution)/shard_map/ppermute | solution.py:25
  9.7 1.3 collective-permute-start.1
  11.0 3.0 %collective-permute-done.1 = f32[3,128]{1,0:T(4,128)S(1)} collective-permute-done((f32[3,128]{1,0:T(4,128)S(1)}, f32[3,128]{1,0:T(4,128)S(1)}, u32[]{:S(2)}, u32[]{:S(2)}) %collective-permute-start.1) | collective-permute-done | bytes 1568 | tf_op jit(solution)/shard_map/ppermute | solution.py:26
  14.0 2.3 %concatenate.42 = f32[1158,128]{1,0:T(8,128)S(1)} concatenate(f32[3,128]{1,0:T(4,128)S(1)} %collective-permute-done, f32[1152,128]{1,0:T(8,128)} %param.5, f32[3,128]{1,0:T(4,128)S(1)} %collective-permute-done.1), dimensions={0} | concatenate | bytes 1185792 | tf_op jit(solution)/shard_map/concatenate | solution.py:27
  16.3 0.2 fusion.57
  16.5 0.2 copy.9
  16.7 3.3 %collective-permute-start.3 = (f32[1158,3]{0,1:T(4,128)S(1)}, f32[1158,3]{0,1:T(4,128)S(1)}, u32[]{:S(2)}, u32[]{:S(2)}) collective-permute-start(f32[1158,3]{0,1:T(4,128)S(1)} %copy.9), channel_id=1, source_target_pairs={{1,0},{2,1},{3,2},{4,3},{5,4},{6,5},{7,6},{9,8},{10,9},{11,10},{12... | collective-permute-start | bytes 41696 | tf_op jit(solution)/shard_map/ppermute | solution.py:26
  20.0 0.2 copy.8
  20.2 2.5 %collective-permute-start.2 = (f32[1158,3]{0,1:T(4,128)S(1)}, f32[1158,3]{0,1:T(4,128)S(1)}, u32[]{:S(2)}, u32[]{:S(2)}) collective-permute-start(f32[1158,3]{0,1:T(4,128)S(1)} %copy.8), channel_id=1, source_target_pairs={{0,1},{1,2},{2,3},{3,4},{4,5},{5,6},{6,7},{8,9},{9,10},{10,11},{11... | collective-permute-start | bytes 41696 | tf_op jit(solution)/shard_map/ppermute | solution.py:25
  22.8 0.2 copy.11
  23.1 3.8 %collective-permute-done.2 = f32[1158,3]{0,1:T(4,128)S(1)} collective-permute-done((f32[1158,3]{0,1:T(4,128)S(1)}, f32[1158,3]{0,1:T(4,128)S(1)}, u32[]{:S(2)}, u32[]{:S(2)}) %collective-permute-start.2) | collective-permute-done | bytes 13928 | tf_op jit(solution)/shard_map/ppermute | solution.py:25
  26.8 0.2 copy.10
  27.1 0.5 pad_maximum_fusion.1
  27.6 0.7 fusion.4
  28.3 1.3 fusion
  29.6 0.7 multiply_bitcast_fusion.1
  30.3 1.6 pad_maximum_fusion
  31.9 0.8 copy-done
  32.8 1.9 %collective-permute-start.5 = (f32[3,1,512]{2,1,0:T(1,128)S(1)}, f32[3,1,512]{2,1,0:T(1,128)S(1)}, u32[]{:S(2)}, u32[]{:S(2)}) collective-permute-start(f32[3,1,512]{2,1,0:T(1,128)S(1)} %get-tuple-element.65), channel_id=1, source_target_pairs={{1,0},{2,1},{3,2},{4,3},{5,4},{6,5},{7,6},{9,8},{10,9},{11,10},{12... | collective-permute-start | bytes 18440 | tf_op jit(solution)/shard_map/ppermute | solution.py:26
  34.7 3.9 %collective-permute-start.4 = (f32[3,1,512]{2,1,0:T(1,128)S(1)}, f32[3,1,512]{2,1,0:T(1,128)S(1)}, u32[]{:S(2)}, u32[]{:S(2)}) collective-permute-start(f32[3,1,512]{2,1,0:T(1,128)S(1)} %get-tuple-element.64), channel_id=1, source_target_pairs={{0,1},{1,2},{2,3},{3,4},{4,5},{5,6},{6,7},{8,9},{9,10},{10,11},{11... | collective-permute-start | bytes 18440 | tf_op jit(solution)/shard_map/ppermute | solution.py:25
  40.0 1.1 collective-permute-done.4
  41.1 0.2 select_maximum_fusion.12
  41.3 0.1 add_bitcast_fusion.7
  41.6 55.6 %all-gather.2.cloned.1.call-done = f32[4,4608,128]{2,1,0:T(8,128)} async-done(((f32[4,1152,128]{2,1,0:T(8,128)}), f32[4,4608,128]{2,1,0:T(8,128)}) %all-gather.2.cloned.1.call-update) | async-done | bytes 9437200 | tf_op jit(solution)/shard_map/all_gather | solution.py:112
  97.2 1.1 constant_dynamic-slice_fusion
  98.3 0.8 copy.12
  99.1 6.0 %all-to-all-start = ((f32[4,8,32,128]{3,2,0,1:T(8,128)}), f32[4,8,32,128]{3,2,0,1:T(8,128)S(1)}, u32[]{:S(2)}, u32[]{:S(2)}) async-start(f32[4,8,32,128]{3,2,0,1:T(8,128)} %copy.12), calls=%async_computation | async-start | bytes 1048576 | tf_op jit(solution)/shard_map/all_to_all | solution.py:115
  105.2 0.1 fusion.52
  105.3 0.2 fusion.31
  105.5 0.2 fusion.28
  105.7 0.1 fusion.44
  105.8 11.5 %all-to-all-done = f32[4,8,32,128]{3,2,0,1:T(8,128)S(1)} async-done(((f32[4,8,32,128]{3,2,0,1:T(8,128)}), f32[4,8,32,128]{3,2,0,1:T(8,128)S(1)}, u32[]{:S(2)}, u32[]{:S(2)}) %all-to-all-start) | async-done | bytes 524320 | tf_op jit(solution)/shard_map/all_to_all | solution.py:115
  117.3 0.3 copy.13
  117.7 0.2 fusion.56
  117.9 2.9 %collective-permute-start.7 = (f32[3,1,512]{2,1,0:T(1,128)S(1)}, f32[3,1,512]{2,1,0:T(1,128)S(1)}, u32[]{:S(2)}, u32[]{:S(2)}) collective-permute-start(f32[3,1,512]{2,1,0:T(1,128)S(1)} %get-tuple-element.62), channel_id=1, source_target_pairs={{1,0},{2,1},{3,2},{4,3},{5,4},{6,5},{7,6},{9,8},{10,9},{11,10},{12... | collective-permute-start | bytes 18440 | tf_op jit(solution)/shard_map/ppermute | solution.py:26
  120.8 3.0 %collective-permute-start.6 = (f32[3,1,512]{2,1,0:T(1,128)S(1)}, f32[3,1,512]{2,1,0:T(1,128)S(1)}, u32[]{:S(2)}, u32[]{:S(2)}) collective-permute-start(f32[3,1,512]{2,1,0:T(1,128)S(1)} %get-tuple-element.61), channel_id=1, source_target_pairs={{0,1},{1,2},{2,3},{3,4},{4,5},{5,6},{6,7},{8,9},{9,10},{10,11},{11... | collective-permute-start | bytes 18440 | tf_op jit(solution)/shard_map/ppermute | solution.py:25
  123.8 3.4 %collective-permute-done.6 = f32[3,1,512]{2,1,0:T(1,128)S(1)} collective-permute-done((f32[3,1,512]{2,1,0:T(1,128)S(1)}, f32[3,1,512]{2,1,0:T(1,128)S(1)}, u32[]{:S(2)}, u32[]{:S(2)}) %collective-permute-start.6) | collective-permute-done | bytes 6176 | tf_op jit(solution)/shard_map/ppermute | solution.py:25
  127.2 0.2 select_maximum_fusion.8
  127.4 0.1 add_bitcast_fusion.5
  127.6 0.1 fusion.50
  127.8 0.2 fusion.23
  128.0 0.2 fusion.26
  128.2 0.1 fusion.42
  128.4 0.2 fusion.53
  128.6 3.7 %collective-permute-start.9 = (f32[3,1,512]{2,1,0:T(1,128)S(1)}, f32[3,1,512]{2,1,0:T(1,128)S(1)}, u32[]{:S(2)}, u32[]{:S(2)}) collective-permute-start(f32[3,1,512]{2,1,0:T(1,128)S(1)} %get-tuple-element.59), channel_id=1, source_target_pairs={{1,0},{2,1},{3,2},{4,3},{5,4},{6,5},{7,6},{9,8},{10,9},{11,10},{12... | collective-permute-start | bytes 18440 | tf_op jit(solution)/shard_map/ppermute | solution.py:26
  132.3 2.1 %collective-permute-start.8 = (f32[3,1,512]{2,1,0:T(1,128)S(1)}, f32[3,1,512]{2,1,0:T(1,128)S(1)}, u32[]{:S(2)}, u32[]{:S(2)}) collective-permute-start(f32[3,1,512]{2,1,0:T(1,128)S(1)} %get-tuple-element.58), channel_id=1, source_target_pairs={{0,1},{1,2},{2,3},{3,4},{4,5},{5,6},{6,7},{8,9},{9,10},{10,11},{11... | collective-permute-start | bytes 18440 | tf_op jit(solution)/shard_map/ppermute | solution.py:25
  134.5 4.3 %collective-permute-done.8 = f32[3,1,512]{2,1,0:T(1,128)S(1)} collective-permute-done((f32[3,1,512]{2,1,0:T(1,128)S(1)}, f32[3,1,512]{2,1,0:T(1,128)S(1)}, u32[]{:S(2)}, u32[]{:S(2)}) %collective-permute-start.8) | collective-permute-done | bytes 6176 | tf_op jit(solution)/shard_map/ppermute | solution.py:25
  138.8 0.2 select_maximum_fusion.4
  139.2 0.1 fusion.48
  139.3 0.2 fusion.18
  139.6 0.2 fusion.21
  139.8 0.1 fusion.40
  139.9 0.2 fusion.54
  140.1 3.9 %collective-permute-start.11 = (f32[3,1,512]{2,1,0:T(1,128)S(1)}, f32[3,1,512]{2,1,0:T(1,128)S(1)}, u32[]{:S(2)}, u32[]{:S(2)}) collective-permute-start(f32[3,1,512]{2,1,0:T(1,128)S(1)} %get-tuple-element.56), channel_id=1, source_target_pairs={{1,0},{2,1},{3,2},{4,3},{5,4},{6,5},{7,6},{9,8},{10,9},{11,10},{12... | collective-permute-start | bytes 18440 | tf_op jit(solution)/shard_map/ppermute | solution.py:26
  144.1 1.9 %collective-permute-start.10 = (f32[3,1,512]{2,1,0:T(1,128)S(1)}, f32[3,1,512]{2,1,0:T(1,128)S(1)}, u32[]{:S(2)}, u32[]{:S(2)}) collective-permute-start(f32[3,1,512]{2,1,0:T(1,128)S(1)} %get-tuple-element.55), channel_id=1, source_target_pairs={{0,1},{1,2},{2,3},{3,4},{4,5},{5,6},{6,7},{8,9},{9,10},{10,11},{11... | collective-permute-start | bytes 18440 | tf_op jit(solution)/shard_map/ppermute | solution.py:25
  146.0 4.5 %collective-permute-done.10 = f32[3,1,512]{2,1,0:T(1,128)S(1)} collective-permute-done((f32[3,1,512]{2,1,0:T(1,128)S(1)}, f32[3,1,512]{2,1,0:T(1,128)S(1)}, u32[]{:S(2)}, u32[]{:S(2)}) %collective-permute-start.10) | collective-permute-done | bytes 6176 | tf_op jit(solution)/shard_map/ppermute | solution.py:25
  150.5 0.2 select_maximum_fusion
  150.9 0.1 fusion.46
  151.0 0.2 fusion.13
  151.3 0.2 fusion.16
  151.5 0.1 fusion.38
  151.6 0.2 fusion.55
  151.8 0.7 maximum_bitcast_fusion
  (38 shorter events, 1.2 us)
Async XLA Ops:
  7.2 90.0 %all-gather.2.cloned.1.call-start = ((), (), s32[]{:S(2)}) async-start(), calls=%async_computation.1 | async-start | bytes 11796480 | tf_op jit(solution)/shard_map/all_gather | solution.py:112
  7.9 3.0 %collective-permute-start = (f32[3,128]{1,0:T(4,128)S(1)}, f32[3,128]{1,0:T(4,128)S(1)}, u32[]{:S(2)}, u32[]{:S(2)}) collective-permute-start(f32[3,128]{1,0:T(4,128)S(1)} %get-tuple-element.21), channel_id=1, source_target_pairs={{0,8},{8,16},{16,24},{1,9},{9,17},{17,25},{2,10},{10,18},{18,26},{... | collective-permute-start | bytes 4616 | tf_op jit(solution)/shard_map/ppermute | solution.py:25
  9.7 4.3 %collective-permute-start.1 = (f32[3,128]{1,0:T(4,128)S(1)}, f32[3,128]{1,0:T(4,128)S(1)}, u32[]{:S(2)}, u32[]{:S(2)}) collective-permute-start(f32[3,128]{1,0:T(4,128)S(1)} %get-tuple-element.20), channel_id=1, source_target_pairs={{8,0},{16,8},{24,16},{9,1},{17,9},{25,17},{10,2},{18,10},{26,18},{... | collective-permute-start | bytes 4616 | tf_op jit(solution)/shard_map/ppermute | solution.py:26
  16.7 6.1 %collective-permute-start.3 = (f32[1158,3]{0,1:T(4,128)S(1)}, f32[1158,3]{0,1:T(4,128)S(1)}, u32[]{:S(2)}, u32[]{:S(2)}) collective-permute-start(f32[1158,3]{0,1:T(4,128)S(1)} %copy.9), channel_id=1, source_target_pairs={{1,0},{2,1},{3,2},{4,3},{5,4},{6,5},{7,6},{9,8},{10,9},{11,10},{12... | collective-permute-start | bytes 41696 | tf_op jit(solution)/shard_map/ppermute | solution.py:26
  20.2 6.6 %collective-permute-start.2 = (f32[1158,3]{0,1:T(4,128)S(1)}, f32[1158,3]{0,1:T(4,128)S(1)}, u32[]{:S(2)}, u32[]{:S(2)}) collective-permute-start(f32[1158,3]{0,1:T(4,128)S(1)} %copy.8), channel_id=1, source_target_pairs={{0,1},{1,2},{2,3},{3,4},{4,5},{5,6},{6,7},{8,9},{9,10},{10,11},{11... | collective-permute-start | bytes 41696 | tf_op jit(solution)/shard_map/ppermute | solution.py:25
  31.9 0.8 copy-start
  31.9 0.9 copy-start.1
  32.8 7.2 %collective-permute-start.5 = (f32[3,1,512]{2,1,0:T(1,128)S(1)}, f32[3,1,512]{2,1,0:T(1,128)S(1)}, u32[]{:S(2)}, u32[]{:S(2)}) collective-permute-start(f32[3,1,512]{2,1,0:T(1,128)S(1)} %get-tuple-element.65), channel_id=1, source_target_pairs={{1,0},{2,1},{3,2},{4,3},{5,4},{6,5},{7,6},{9,8},{10,9},{11,10},{12... | collective-permute-start | bytes 18440 | tf_op jit(solution)/shard_map/ppermute | solution.py:26
  34.7 6.4 %collective-permute-start.4 = (f32[3,1,512]{2,1,0:T(1,128)S(1)}, f32[3,1,512]{2,1,0:T(1,128)S(1)}, u32[]{:S(2)}, u32[]{:S(2)}) collective-permute-start(f32[3,1,512]{2,1,0:T(1,128)S(1)} %get-tuple-element.64), channel_id=1, source_target_pairs={{0,1},{1,2},{2,3},{3,4},{4,5},{5,6},{6,7},{8,9},{9,10},{10,11},{11... | collective-permute-start | bytes 18440 | tf_op jit(solution)/shard_map/ppermute | solution.py:25
  99.1 18.2 %all-to-all-start = ((f32[4,8,32,128]{3,2,0,1:T(8,128)}), f32[4,8,32,128]{3,2,0,1:T(8,128)S(1)}, u32[]{:S(2)}, u32[]{:S(2)}) async-start(f32[4,8,32,128]{3,2,0,1:T(8,128)} %copy.12), calls=%async_computation | async-start | bytes 1048576 | tf_op jit(solution)/shard_map/all_to_all | solution.py:115
  117.9 5.9 %collective-permute-start.7 = (f32[3,1,512]{2,1,0:T(1,128)S(1)}, f32[3,1,512]{2,1,0:T(1,128)S(1)}, u32[]{:S(2)}, u32[]{:S(2)}) collective-permute-start(f32[3,1,512]{2,1,0:T(1,128)S(1)} %get-tuple-element.62), channel_id=1, source_target_pairs={{1,0},{2,1},{3,2},{4,3},{5,4},{6,5},{7,6},{9,8},{10,9},{11,10},{12... | collective-permute-start | bytes 18440 | tf_op jit(solution)/shard_map/ppermute | solution.py:26
  120.8 6.4 %collective-permute-start.6 = (f32[3,1,512]{2,1,0:T(1,128)S(1)}, f32[3,1,512]{2,1,0:T(1,128)S(1)}, u32[]{:S(2)}, u32[]{:S(2)}) collective-permute-start(f32[3,1,512]{2,1,0:T(1,128)S(1)} %get-tuple-element.61), channel_id=1, source_target_pairs={{0,1},{1,2},{2,3},{3,4},{4,5},{5,6},{6,7},{8,9},{9,10},{10,11},{11... | collective-permute-start | bytes 18440 | tf_op jit(solution)/shard_map/ppermute | solution.py:25
  128.6 5.9 %collective-permute-start.9 = (f32[3,1,512]{2,1,0:T(1,128)S(1)}, f32[3,1,512]{2,1,0:T(1,128)S(1)}, u32[]{:S(2)}, u32[]{:S(2)}) collective-permute-start(f32[3,1,512]{2,1,0:T(1,128)S(1)} %get-tuple-element.59), channel_id=1, source_target_pairs={{1,0},{2,1},{3,2},{4,3},{5,4},{6,5},{7,6},{9,8},{10,9},{11,10},{12... | collective-permute-start | bytes 18440 | tf_op jit(solution)/shard_map/ppermute | solution.py:26
  132.3 6.4 %collective-permute-start.8 = (f32[3,1,512]{2,1,0:T(1,128)S(1)}, f32[3,1,512]{2,1,0:T(1,128)S(1)}, u32[]{:S(2)}, u32[]{:S(2)}) collective-permute-start(f32[3,1,512]{2,1,0:T(1,128)S(1)} %get-tuple-element.58), channel_id=1, source_target_pairs={{0,1},{1,2},{2,3},{3,4},{4,5},{5,6},{6,7},{8,9},{9,10},{10,11},{11... | collective-permute-start | bytes 18440 | tf_op jit(solution)/shard_map/ppermute | solution.py:25
  140.1 5.9 %collective-permute-start.11 = (f32[3,1,512]{2,1,0:T(1,128)S(1)}, f32[3,1,512]{2,1,0:T(1,128)S(1)}, u32[]{:S(2)}, u32[]{:S(2)}) collective-permute-start(f32[3,1,512]{2,1,0:T(1,128)S(1)} %get-tuple-element.56), channel_id=1, source_target_pairs={{1,0},{2,1},{3,2},{4,3},{5,4},{6,5},{7,6},{9,8},{10,9},{11,10},{12... | collective-permute-start | bytes 18440 | tf_op jit(solution)/shard_map/ppermute | solution.py:26
  144.1 6.4 %collective-permute-start.10 = (f32[3,1,512]{2,1,0:T(1,128)S(1)}, f32[3,1,512]{2,1,0:T(1,128)S(1)}, u32[]{:S(2)}, u32[]{:S(2)}) collective-permute-start(f32[3,1,512]{2,1,0:T(1,128)S(1)} %get-tuple-element.55), channel_id=1, source_target_pairs={{0,1},{1,2},{2,3},{3,4},{4,5},{5,6},{6,7},{8,9},{9,10},{10,11},{11... | collective-permute-start | bytes 18440 | tf_op jit(solution)/shard_map/ppermute | solution.py:25
Sparse Core Ops, SparseCore 0:
  32.0 65.1 all-gather.1
where the time goes:
time: 160 us; the launch traced here: 159 us
  waiting for transfers between devices  87.3 us (55%)
  starting transfers between devices  38.3 us (24%)
  between operations  15.9 us (10%)
  other arithmetic  10.6 us (7%)
  local copies, waits for them, and re-layouts  7.37 us (5%)
    all_gather x1, waiting for transfers between devices, shards(): column_strip = lax.all_gather(ground_geometry, 'grp', axis=1, tiled=True)  55.6 us
    ppermute x6, waiting for transfers between devices, padded(): before = lax.ppermute(last, axis, up)  17.1 us
    ppermute x6, starting transfers between devices, padded(): after = lax.ppermute(leading, axis, down)  17.1 us
    ppermute x6, starting transfers between devices, padded(): before = lax.ppermute(last, axis, up)  15.2 us
    all_to_all x1, waiting for transfers between devices, shards(): lax.all_to_all(blocks, 'tile', split_axis=1, concat_axis=3, tiled=True)  11.5 us
    all_to_all x1, starting transfers between devices, shards(): lax.all_to_all(blocks, 'tile', split_axis=1, concat_axis=3, tiled=True)  6.03 us
  transfers between devices with their start and end apart: 14, of which 8 were waited for; matrix products, arithmetic and copies ran while one was open for 1% of the time, Pallas kernels for 0%

commit v1 on v0

--- a/solution.py
+++ b/solution.py
@@ -13,6 +13,29 @@
 depth_floor = 0.1
 speed_floor = 0.5
 binomial = (0.0625, 0.25, 0.375, 0.25, 0.0625)
+
+
+def in_blocks(x, dim, size):
+    lengths = x.shape
+    tiles = x.reshape(*lengths[:dim], size, lengths[dim] // size, *lengths[dim + 1 :])
+    return jnp.moveaxis(tiles, dim, 0)
+
+
+def in_order(tiles, dim):
+    tiles = jnp.moveaxis(tiles, 0, dim)
+    shape = tiles.shape
+    return tiles.reshape(*shape[:dim], shape[dim] * shape[dim + 1], *shape[dim + 2 :])
+
+
+def pairwise_exchange(shard, axis, split_dim, concat_dim):
+    size, index = (lax.axis_size(axis), lax.axis_index(axis))
+    tiles = in_blocks(shard, split_dim, size)
+    gathered = [tiles[index]]
+    for hop in range(1, size):
+        sent = tiles[index ^ hop]
+        gathered.append(lax.ppermute(sent, axis, [(i, i ^ hop) for i in range(size)]))
+    tiles = jnp.stack(gathered)[index ^ jnp.arange(size)]
+    return in_order(tiles, concat_dim)
 
 
 def padded(shard, sides, width):
@@ -112,7 +135,7 @@
     column_strip = lax.all_gather(ground_geometry, "grp", axis=1, tiled=True)
     row_band = lax.dynamic_slice_in_dim(column_strip, first_row, window_height, 1)
     blocks = row_band.reshape(4, tile_count, piece_rows, block_lateral_number)
-    rows_wide = lax.all_to_all(blocks, "tile", split_axis=1, concat_axis=3, tiled=True)
+    rows_wide = pairwise_exchange(blocks, "tile", 1, 3)
     rows_wide = rows_wide.reshape(4, piece_rows, tile_count * block_lateral_number)
     under_window = lax.dynamic_slice_in_dim(rows_wide, first_col, window_width, 2)
     release_depth = (

time: 160 us -> 157 us (0.981)
  waiting for transfers between devices: 87.3 us -> 80.2 us
  starting transfers between devices: 38.3 us -> 41.8 us
    all_to_all x1 -> x0, waiting for transfers between devices: 11.5 us -> none  [shards(): lax.all_to_all(blocks, 'tile', split_axis=1, concat_axis=3, tiled=True)]
    ppermute x0 -> x7, starting transfers between devices: none -> 9.53 us  [pairwise_exchange(): lax.ppermute(sent, axis, [(i, i ^ hop) for i in range(size)])]
    ppermute x0 -> x7, waiting for transfers between devices: none -> 9 us  [pairwise_exchange(): lax.ppermute(sent, axis, [(i, i ^ hop) for i in range(size)])]
    all_to_all x1 -> x0, starting transfers between devices: 6.03 us -> none  [shards(): lax.all_to_all(blocks, 'tile', split_axis=1, concat_axis=3, tiled=True)]
    ppermute x6, waiting for transfers between devices: 17.1 us -> 13.2 us  [padded(): before = lax.ppermute(last, axis, up)]
    ppermute x6, starting transfers between devices: 17.1 us -> 13.2 us  [padded(): after = lax.ppermute(leading, axis, down)]
    ppermute x6, starting transfers between devices: 15.2 us -> 19 us  [padded(): before = lax.ppermute(last, axis, up)]
  transfers between devices with their start and end apart: 14 -> 20, of which waited for: 8 -> 10; matrix products, arithmetic and copies ran while one was open for 1% -> 1% of each run, Pallas kernels for 0% -> 0%
where the time goes in v1:
time: 157 us; the launch traced here: 156 us
  waiting for transfers between devices  80.2 us (51%)
  starting transfers between devices  41.8 us (27%)
  between operations  16 us (10%)
  other arithmetic  10.6 us (7%)
  local copies, waits for them, and re-layouts  7.21 us (5%)
    all_gather x1, waiting for transfers between devices, shards(): column_strip = lax.all_gather(ground_geometry, 'grp', axis=1, tiled=True)  54.9 us
    ppermute x6, starting transfers between devices, padded(): before = lax.ppermute(last, axis, up)  19 us
    ppermute x6, starting transfers between devices, padded(): after = lax.ppermute(leading, axis, down)  13.2 us
    ppermute x6, waiting for transfers between devices, padded(): before = lax.ppermute(last, axis, up)  13.2 us
    ppermute x7, starting transfers between devices, pairwise_exchange(): lax.ppermute(sent, axis, [(i, i ^ hop) for i in range(size)])  9.53 us
    ppermute x7, waiting for transfers between devices, pairwise_exchange(): lax.ppermute(sent, axis, [(i, i ^ hop) for i in range(size)])  9 us
  transfers between devices with their start and end apart: 20, of which 10 were waited for; matrix products, arithmetic and copies ran while one was open for 1% of the time, Pallas kernels for 0%

profile of v1, /device:TPU:16, one launch (start us, length us, event | category | flops | bytes accessed | tf_op | source)
XLA Modules:
  0.0 155.8 jit_solution(16617698468363125629)
XLA Ops:
  7.2 0.7 fusion.59
  7.9 1.7 %collective-permute-start = (f32[3,128]{1,0:T(4,128)S(1)}, f32[3,128]{1,0:T(4,128)S(1)}, u32[]{:S(2)}, u32[]{:S(2)}) collective-permute-start(f32[3,128]{1,0:T(4,128)S(1)} %get-tuple-element.21), channel_id=1, source_target_pairs={{0,8},{8,16},{16,24},{1,9},{9,17},{17,25},{2,10},{10,18},{18,26},{... | collective-permute-start | bytes 4616 | tf_op jit(solution)/shard_map/ppermute | solution.py:48
  9.7 1.3 collective-permute-start.1
  11.0 3.0 %collective-permute-done.1 = f32[3,128]{1,0:T(4,128)S(1)} collective-permute-done((f32[3,128]{1,0:T(4,128)S(1)}, f32[3,128]{1,0:T(4,128)S(1)}, u32[]{:S(2)}, u32[]{:S(2)}) %collective-permute-start.1) | collective-permute-done | bytes 1568 | tf_op jit(solution)/shard_map/ppermute | solution.py:49
  14.0 2.3 %concatenate.42 = f32[1158,128]{1,0:T(8,128)S(1)} concatenate(f32[3,128]{1,0:T(4,128)S(1)} %collective-permute-done, f32[1152,128]{1,0:T(8,128)} %param.5, f32[3,128]{1,0:T(4,128)S(1)} %collective-permute-done.1), dimensions={0} | concatenate | bytes 1185792 | tf_op jit(solution)/shard_map/concatenate | solution.py:50
  16.3 0.2 fusion.58
  16.5 0.2 copy.9
  16.7 3.3 %collective-permute-start.3 = (f32[1158,3]{0,1:T(4,128)S(1)}, f32[1158,3]{0,1:T(4,128)S(1)}, u32[]{:S(2)}, u32[]{:S(2)}) collective-permute-start(f32[1158,3]{0,1:T(4,128)S(1)} %copy.9), channel_id=1, source_target_pairs={{1,0},{2,1},{3,2},{4,3},{5,4},{6,5},{7,6},{9,8},{10,9},{11,10},{12... | collective-permute-start | bytes 41696 | tf_op jit(solution)/shard_map/ppermute | solution.py:49
  20.0 0.2 copy.8
  20.2 2.5 %collective-permute-start.2 = (f32[1158,3]{0,1:T(4,128)S(1)}, f32[1158,3]{0,1:T(4,128)S(1)}, u32[]{:S(2)}, u32[]{:S(2)}) collective-permute-start(f32[1158,3]{0,1:T(4,128)S(1)} %copy.8), channel_id=1, source_target_pairs={{0,1},{1,2},{2,3},{3,4},{4,5},{5,6},{6,7},{8,9},{9,10},{10,11},{11... | collective-permute-start | bytes 41696 | tf_op jit(solution)/shard_map/ppermute | solution.py:48
  22.8 0.2 copy.11
  23.1 3.8 %collective-permute-done.2 = f32[1158,3]{0,1:T(4,128)S(1)} collective-permute-done((f32[1158,3]{0,1:T(4,128)S(1)}, f32[1158,3]{0,1:T(4,128)S(1)}, u32[]{:S(2)}, u32[]{:S(2)}) %collective-permute-start.2) | collective-permute-done | bytes 13928 | tf_op jit(solution)/shard_map/ppermute | solution.py:48
  26.8 0.2 copy.10
  27.1 0.5 pad_maximum_fusion.1
  27.6 0.7 fusion.4
  28.3 1.3 fusion
  29.6 0.7 multiply_bitcast_fusion.1
  30.3 1.6 %pad_maximum_fusion = f32[4,1152,128]{2,1,0:T(8,128)} fusion(f32[1,1152,128]{2,1,0:T(8,128)S(1)} %get-tuple-element.16, f32[1,1152,128]{2,1,0:T(8,128)S(1)} %get-tuple-element.15, f32[1,1152,128]{2,1,0:T(8,128)S(1)} %get-tuple-element.17, f32[1,1152,128]{2,1,0:T(8,128)S(1)} %get-tuple-element.14), kind=kLoop, calls=%fused_computation.1 | loop fusion | flops 1769472 | bytes 4718592 | tf_op jit(solution)/shard_map/stack | solution.py:76
  31.9 0.8 copy-done
  32.8 1.9 %collective-permute-start.5 = (f32[3,1,512]{2,1,0:T(1,128)S(1)}, f32[3,1,512]{2,1,0:T(1,128)S(1)}, u32[]{:S(2)}, u32[]{:S(2)}) collective-permute-start(f32[3,1,512]{2,1,0:T(1,128)S(1)} %get-tuple-element.72), channel_id=1, source_target_pairs={{1,0},{2,1},{3,2},{4,3},{5,4},{6,5},{7,6},{9,8},{10,9},{11,10},{12... | collective-permute-start | bytes 18440 | tf_op jit(solution)/shard_map/ppermute | solution.py:49
  34.7 3.9 %collective-permute-start.4 = (f32[3,1,512]{2,1,0:T(1,128)S(1)}, f32[3,1,512]{2,1,0:T(1,128)S(1)}, u32[]{:S(2)}, u32[]{:S(2)}) collective-permute-start(f32[3,1,512]{2,1,0:T(1,128)S(1)} %get-tuple-element.71), channel_id=1, source_target_pairs={{0,1},{1,2},{2,3},{3,4},{4,5},{5,6},{6,7},{8,9},{9,10},{10,11},{11... | collective-permute-start | bytes 18440 | tf_op jit(solution)/shard_map/ppermute | solution.py:48
  40.1 1.0 collective-permute-done.4
  41.1 0.2 select_maximum_fusion.12
  41.7 0.2 fusion.31
  41.9 0.2 fusion.28
  42.2 54.9 %all-gather.2.cloned.1.call-done = f32[4,4608,128]{2,1,0:T(8,128)} async-done(((f32[4,1152,128]{2,1,0:T(8,128)}), f32[4,4608,128]{2,1,0:T(8,128)}) %all-gather.2.cloned.1.call-update) | async-done | bytes 9437200 | tf_op jit(solution)/shard_map/all_gather | solution.py:135
  97.2 1.1 constant_dynamic-slice_fusion
  98.3 1.5 collective-permute-start.6
  99.9 1.5 collective-permute-start.7
  101.4 0.5 collective-permute-start.8
  101.9 0.5 collective-permute-start.9
  102.4 3.3 %collective-permute-start.10 = (f32[4,1,32,128]{3,2,0,1:T(8,128)S(1)}, f32[4,1,32,128]{3,2,0,1:T(8,128)S(1)}, u32[]{:S(2)}, u32[]{:S(2)}) collective-permute-start(f32[4,1,32,128]{3,2,0,1:T(8,128)S(1)} %get-tuple-element.24), channel_id=1, source_target_pairs={{0,5},{1,4},{2,7},{3,6},{4,1},{5,0},{6,3},{7,2},{8,13},{9,12},{10,... | collective-permute-start | bytes 196616 | tf_op jit(solution)/shard_map/ppermute | solution.py:36
  105.7 0.6 collective-permute-start.11
  106.4 1.5 collective-permute-start.12
  108.0 2.9 %collective-permute-done.10 = f32[4,1,32,128]{3,2,0,1:T(8,128)S(1)} collective-permute-done((f32[4,1,32,128]{3,2,0,1:T(8,128)S(1)}, f32[4,1,32,128]{3,2,0,1:T(8,128)S(1)}, u32[]{:S(2)}, u32[]{:S(2)}) %collective-permute-start.10) | collective-permute-done | bytes 65568 | tf_op jit(solution)/shard_map/ppermute | solution.py:36
  110.9 4.4 %collective-permute-done.11 = f32[4,1,32,128]{3,2,0,1:T(8,128)S(1)} collective-permute-done((f32[4,1,32,128]{3,2,0,1:T(8,128)S(1)}, f32[4,1,32,128]{3,2,0,1:T(8,128)S(1)}, u32[]{:S(2)}, u32[]{:S(2)}) %collective-permute-start.11) | collective-permute-done | bytes 65568 | tf_op jit(solution)/shard_map/ppermute | solution.py:36
  115.2 1.7 %collective-permute-done.12 = f32[4,1,32,128]{3,2,0,1:T(8,128)S(1)} collective-permute-done((f32[4,1,32,128]{3,2,0,1:T(8,128)S(1)}, f32[4,1,32,128]{3,2,0,1:T(8,128)S(1)}, u32[]{:S(2)}, u32[]{:S(2)}) %collective-permute-start.12) | collective-permute-done | bytes 65568 | tf_op jit(solution)/shard_map/ppermute | solution.py:36
  117.0 0.6 gather_fusion
  117.5 0.3 copy.12
  118.0 0.2 fusion.57
  118.2 2.5 %collective-permute-start.14 = (f32[3,1,512]{2,1,0:T(1,128)S(1)}, f32[3,1,512]{2,1,0:T(1,128)S(1)}, u32[]{:S(2)}, u32[]{:S(2)}) collective-permute-start(f32[3,1,512]{2,1,0:T(1,128)S(1)} %get-tuple-element.69), channel_id=1, source_target_pairs={{1,0},{2,1},{3,2},{4,3},{5,4},{6,5},{7,6},{9,8},{10,9},{11,10},{12... | collective-permute-start | bytes 18440 | tf_op jit(solution)/shard_map/ppermute | solution.py:49
  120.7 3.3 %collective-permute-start.13 = (f32[3,1,512]{2,1,0:T(1,128)S(1)}, f32[3,1,512]{2,1,0:T(1,128)S(1)}, u32[]{:S(2)}, u32[]{:S(2)}) collective-permute-start(f32[3,1,512]{2,1,0:T(1,128)S(1)} %get-tuple-element.68), channel_id=1, source_target_pairs={{0,1},{1,2},{2,3},{3,4},{4,5},{5,6},{6,7},{8,9},{9,10},{10,11},{11... | collective-permute-start | bytes 18440 | tf_op jit(solution)/shard_map/ppermute | solution.py:48
  124.1 3.1 %collective-permute-done.13 = f32[3,1,512]{2,1,0:T(1,128)S(1)} collective-permute-done((f32[3,1,512]{2,1,0:T(1,128)S(1)}, f32[3,1,512]{2,1,0:T(1,128)S(1)}, u32[]{:S(2)}, u32[]{:S(2)}) %collective-permute-start.13) | collective-permute-done | bytes 6176 | tf_op jit(solution)/shard_map/ppermute | solution.py:48
  127.2 0.2 select_maximum_fusion.8
  127.7 0.2 fusion.23
  127.9 0.2 fusion.26
  128.3 0.2 fusion.54
  128.5 2.2 %collective-permute-start.16 = (f32[3,1,512]{2,1,0:T(1,128)S(1)}, f32[3,1,512]{2,1,0:T(1,128)S(1)}, u32[]{:S(2)}, u32[]{:S(2)}) collective-permute-start(f32[3,1,512]{2,1,0:T(1,128)S(1)} %get-tuple-element.66), channel_id=1, source_target_pairs={{1,0},{2,1},{3,2},{4,3},{5,4},{6,5},{7,6},{9,8},{10,9},{11,10},{12... | collective-permute-start | bytes 18440 | tf_op jit(solution)/shard_map/ppermute | solution.py:49
  130.7 3.7 %collective-permute-start.15 = (f32[3,1,512]{2,1,0:T(1,128)S(1)}, f32[3,1,512]{2,1,0:T(1,128)S(1)}, u32[]{:S(2)}, u32[]{:S(2)}) collective-permute-start(f32[3,1,512]{2,1,0:T(1,128)S(1)} %get-tuple-element.65), channel_id=1, source_target_pairs={{0,1},{1,2},{2,3},{3,4},{4,5},{5,6},{6,7},{8,9},{9,10},{10,11},{11... | collective-permute-start | bytes 18440 | tf_op jit(solution)/shard_map/ppermute | solution.py:48
  134.4 2.7 %collective-permute-done.15 = f32[3,1,512]{2,1,0:T(1,128)S(1)} collective-permute-done((f32[3,1,512]{2,1,0:T(1,128)S(1)}, f32[3,1,512]{2,1,0:T(1,128)S(1)}, u32[]{:S(2)}, u32[]{:S(2)}) %collective-permute-start.15) | collective-permute-done | bytes 6176 | tf_op jit(solution)/shard_map/ppermute | solution.py:48
  137.1 0.2 select_maximum_fusion.4
  137.7 0.2 fusion.18
  137.9 0.2 fusion.21
  138.1 0.1 fusion.40
  138.2 0.2 fusion.55
  138.5 2.0 %collective-permute-start.18 = (f32[3,1,512]{2,1,0:T(1,128)S(1)}, f32[3,1,512]{2,1,0:T(1,128)S(1)}, u32[]{:S(2)}, u32[]{:S(2)}) collective-permute-start(f32[3,1,512]{2,1,0:T(1,128)S(1)} %get-tuple-element.63), channel_id=1, source_target_pairs={{1,0},{2,1},{3,2},{4,3},{5,4},{6,5},{7,6},{9,8},{10,9},{11,10},{12... | collective-permute-start | bytes 18440 | tf_op jit(solution)/shard_map/ppermute | solution.py:49
  140.5 3.8 %collective-permute-start.17 = (f32[3,1,512]{2,1,0:T(1,128)S(1)}, f32[3,1,512]{2,1,0:T(1,128)S(1)}, u32[]{:S(2)}, u32[]{:S(2)}) collective-permute-start(f32[3,1,512]{2,1,0:T(1,128)S(1)} %get-tuple-element.62), channel_id=1, source_target_pairs={{0,1},{1,2},{2,3},{3,4},{4,5},{5,6},{6,7},{8,9},{9,10},{10,11},{11... | collective-permute-start | bytes 18440 | tf_op jit(solution)/shard_map/ppermute | solution.py:48
  144.3 2.6 %collective-permute-done.17 = f32[3,1,512]{2,1,0:T(1,128)S(1)} collective-permute-done((f32[3,1,512]{2,1,0:T(1,128)S(1)}, f32[3,1,512]{2,1,0:T(1,128)S(1)}, u32[]{:S(2)}, u32[]{:S(2)}) %collective-permute-start.17) | collective-permute-done | bytes 6176 | tf_op jit(solution)/shard_map/ppermute | solution.py:48
  146.9 0.2 select_maximum_fusion
  147.5 0.2 fusion.13
  147.7 0.2 fusion.16
  147.9 0.1 fusion.38
  148.0 0.2 fusion.56
  148.2 0.7 maximum_bitcast_fusion
  (61 shorter events, 2.2 us)
Async XLA Ops:
  7.2 90.0 %all-gather.2.cloned.1.call-start = ((), (), s32[]{:S(2)}) async-start(), calls=%async_computation | async-start | bytes 11796480 | tf_op jit(solution)/shard_map/all_gather | solution.py:135
  7.9 3.0 %collective-permute-start = (f32[3,128]{1,0:T(4,128)S(1)}, f32[3,128]{1,0:T(4,128)S(1)}, u32[]{:S(2)}, u32[]{:S(2)}) collective-permute-start(f32[3,128]{1,0:T(4,128)S(1)} %get-tuple-element.21), channel_id=1, source_target_pairs={{0,8},{8,16},{16,24},{1,9},{9,17},{17,25},{2,10},{10,18},{18,26},{... | collective-permute-start | bytes 4616 | tf_op jit(solution)/shard_map/ppermute | solution.py:48
  9.7 4.3 %collective-permute-start.1 = (f32[3,128]{1,0:T(4,128)S(1)}, f32[3,128]{1,0:T(4,128)S(1)}, u32[]{:S(2)}, u32[]{:S(2)}) collective-permute-start(f32[3,128]{1,0:T(4,128)S(1)} %get-tuple-element.20), channel_id=1, source_target_pairs={{8,0},{16,8},{24,16},{9,1},{17,9},{25,17},{10,2},{18,10},{26,18},{... | collective-permute-start | bytes 4616 | tf_op jit(solution)/shard_map/ppermute | solution.py:49
  16.7 6.1 %collective-permute-start.3 = (f32[1158,3]{0,1:T(4,128)S(1)}, f32[1158,3]{0,1:T(4,128)S(1)}, u32[]{:S(2)}, u32[]{:S(2)}) collective-permute-start(f32[1158,3]{0,1:T(4,128)S(1)} %copy.9), channel_id=1, source_target_pairs={{1,0},{2,1},{3,2},{4,3},{5,4},{6,5},{7,6},{9,8},{10,9},{11,10},{12... | collective-permute-start | bytes 41696 | tf_op jit(solution)/shard_map/ppermute | solution.py:49
  20.2 6.6 %collective-permute-start.2 = (f32[1158,3]{0,1:T(4,128)S(1)}, f32[1158,3]{0,1:T(4,128)S(1)}, u32[]{:S(2)}, u32[]{:S(2)}) collective-permute-start(f32[1158,3]{0,1:T(4,128)S(1)} %copy.8), channel_id=1, source_target_pairs={{0,1},{1,2},{2,3},{3,4},{4,5},{5,6},{6,7},{8,9},{9,10},{10,11},{11... | collective-permute-start | bytes 41696 | tf_op jit(solution)/shard_map/ppermute | solution.py:48
  31.9 0.8 copy-start
  31.9 0.9 copy-start.1
  32.8 7.3 %collective-permute-start.5 = (f32[3,1,512]{2,1,0:T(1,128)S(1)}, f32[3,1,512]{2,1,0:T(1,128)S(1)}, u32[]{:S(2)}, u32[]{:S(2)}) collective-permute-start(f32[3,1,512]{2,1,0:T(1,128)S(1)} %get-tuple-element.72), channel_id=1, source_target_pairs={{1,0},{2,1},{3,2},{4,3},{5,4},{6,5},{7,6},{9,8},{10,9},{11,10},{12... | collective-permute-start | bytes 18440 | tf_op jit(solution)/shard_map/ppermute | solution.py:49
  34.7 6.4 %collective-permute-start.4 = (f32[3,1,512]{2,1,0:T(1,128)S(1)}, f32[3,1,512]{2,1,0:T(1,128)S(1)}, u32[]{:S(2)}, u32[]{:S(2)}) collective-permute-start(f32[3,1,512]{2,1,0:T(1,128)S(1)} %get-tuple-element.71), channel_id=1, source_target_pairs={{0,1},{1,2},{2,3},{3,4},{4,5},{5,6},{6,7},{8,9},{9,10},{10,11},{11... | collective-permute-start | bytes 18440 | tf_op jit(solution)/shard_map/ppermute | solution.py:48
  98.3 7.4 %collective-permute-start.6 = (f32[4,1,32,128]{3,2,0,1:T(8,128)S(1)}, f32[4,1,32,128]{3,2,0,1:T(8,128)S(1)}, u32[]{:S(2)}, u32[]{:S(2)}) collective-permute-start(f32[4,1,32,128]{3,2,0,1:T(8,128)S(1)} %get-tuple-element.28), channel_id=1, source_target_pairs={{0,1},{1,0},{2,3},{3,2},{4,5},{5,4},{6,7},{7,6},{8,9},{9,8},{10,11... | collective-permute-start | bytes 196616 | tf_op jit(solution)/shard_map/ppermute | solution.py:36
  99.9 6.5 %collective-permute-start.7 = (f32[4,1,32,128]{3,2,0,1:T(8,128)S(1)}, f32[4,1,32,128]{3,2,0,1:T(8,128)S(1)}, u32[]{:S(2)}, u32[]{:S(2)}) collective-permute-start(f32[4,1,32,128]{3,2,0,1:T(8,128)S(1)} %get-tuple-element.27), channel_id=1, source_target_pairs={{0,2},{1,3},{2,0},{3,1},{4,6},{5,7},{6,4},{7,5},{8,10},{9,11},{10,... | collective-permute-start | bytes 196616 | tf_op jit(solution)/shard_map/ppermute | solution.py:36
  101.4 6.5 %collective-permute-start.8 = (f32[4,1,32,128]{3,2,0,1:T(8,128)S(1)}, f32[4,1,32,128]{3,2,0,1:T(8,128)S(1)}, u32[]{:S(2)}, u32[]{:S(2)}) collective-permute-start(f32[4,1,32,128]{3,2,0,1:T(8,128)S(1)} %get-tuple-element.26), channel_id=1, source_target_pairs={{0,3},{1,2},{2,1},{3,0},{4,7},{5,6},{6,5},{7,4},{8,11},{9,10},{10,... | collective-permute-start | bytes 196616 | tf_op jit(solution)/shard_map/ppermute | solution.py:36
  101.9 6.0 %collective-permute-start.9 = (f32[4,1,32,128]{3,2,0,1:T(8,128)S(1)}, f32[4,1,32,128]{3,2,0,1:T(8,128)S(1)}, u32[]{:S(2)}, u32[]{:S(2)}) collective-permute-start(f32[4,1,32,128]{3,2,0,1:T(8,128)S(1)} %get-tuple-element.25), channel_id=1, source_target_pairs={{0,4},{1,5},{2,6},{3,7},{4,0},{5,1},{6,2},{7,3},{8,12},{9,13},{10,... | collective-permute-start | bytes 196616 | tf_op jit(solution)/shard_map/ppermute | solution.py:36
  102.4 8.4 %collective-permute-start.10 = (f32[4,1,32,128]{3,2,0,1:T(8,128)S(1)}, f32[4,1,32,128]{3,2,0,1:T(8,128)S(1)}, u32[]{:S(2)}, u32[]{:S(2)}) collective-permute-start(f32[4,1,32,128]{3,2,0,1:T(8,128)S(1)} %get-tuple-element.24), channel_id=1, source_target_pairs={{0,5},{1,4},{2,7},{3,6},{4,1},{5,0},{6,3},{7,2},{8,13},{9,12},{10,... | collective-permute-start | bytes 196616 | tf_op jit(solution)/shard_map/ppermute | solution.py:36
  105.7 9.5 %collective-permute-start.11 = (f32[4,1,32,128]{3,2,0,1:T(8,128)S(1)}, f32[4,1,32,128]{3,2,0,1:T(8,128)S(1)}, u32[]{:S(2)}, u32[]{:S(2)}) collective-permute-start(f32[4,1,32,128]{3,2,0,1:T(8,128)S(1)} %get-tuple-element.23), channel_id=1, source_target_pairs={{0,6},{1,7},{2,4},{3,5},{4,2},{5,3},{6,0},{7,1},{8,14},{9,15},{10,... | collective-permute-start | bytes 196616 | tf_op jit(solution)/shard_map/ppermute | solution.py:36
  106.4 10.6 %collective-permute-start.12 = (f32[4,1,32,128]{3,2,0,1:T(8,128)S(1)}, f32[4,1,32,128]{3,2,0,1:T(8,128)S(1)}, u32[]{:S(2)}, u32[]{:S(2)}) collective-permute-start(f32[4,1,32,128]{3,2,0,1:T(8,128)S(1)} %get-tuple-element.22), channel_id=1, source_target_pairs={{0,7},{1,6},{2,5},{3,4},{4,3},{5,2},{6,1},{7,0},{8,15},{9,14},{10,... | collective-permute-start | bytes 196616 | tf_op jit(solution)/shard_map/ppermute | solution.py:36
  118.2 5.9 %collective-permute-start.14 = (f32[3,1,512]{2,1,0:T(1,128)S(1)}, f32[3,1,512]{2,1,0:T(1,128)S(1)}, u32[]{:S(2)}, u32[]{:S(2)}) collective-permute-start(f32[3,1,512]{2,1,0:T(1,128)S(1)} %get-tuple-element.69), channel_id=1, source_target_pairs={{1,0},{2,1},{3,2},{4,3},{5,4},{6,5},{7,6},{9,8},{10,9},{11,10},{12... | collective-permute-start | bytes 18440 | tf_op jit(solution)/shard_map/ppermute | solution.py:49
  120.7 6.4 %collective-permute-start.13 = (f32[3,1,512]{2,1,0:T(1,128)S(1)}, f32[3,1,512]{2,1,0:T(1,128)S(1)}, u32[]{:S(2)}, u32[]{:S(2)}) collective-permute-start(f32[3,1,512]{2,1,0:T(1,128)S(1)} %get-tuple-element.68), channel_id=1, source_target_pairs={{0,1},{1,2},{2,3},{3,4},{4,5},{5,6},{6,7},{8,9},{9,10},{10,11},{11... | collective-permute-start | bytes 18440 | tf_op jit(solution)/shard_map/ppermute | solution.py:48
  128.5 5.9 %collective-permute-start.16 = (f32[3,1,512]{2,1,0:T(1,128)S(1)}, f32[3,1,512]{2,1,0:T(1,128)S(1)}, u32[]{:S(2)}, u32[]{:S(2)}) collective-permute-start(f32[3,1,512]{2,1,0:T(1,128)S(1)} %get-tuple-element.66), channel_id=1, source_target_pairs={{1,0},{2,1},{3,2},{4,3},{5,4},{6,5},{7,6},{9,8},{10,9},{11,10},{12... | collective-permute-start | bytes 18440 | tf_op jit(solution)/shard_map/ppermute | solution.py:49
  130.7 6.4 %collective-permute-start.15 = (f32[3,1,512]{2,1,0:T(1,128)S(1)}, f32[3,1,512]{2,1,0:T(1,128)S(1)}, u32[]{:S(2)}, u32[]{:S(2)}) collective-permute-start(f32[3,1,512]{2,1,0:T(1,128)S(1)} %get-tuple-element.65), channel_id=1, source_target_pairs={{0,1},{1,2},{2,3},{3,4},{4,5},{5,6},{6,7},{8,9},{9,10},{10,11},{11... | collective-permute-start | bytes 18440 | tf_op jit(solution)/shard_map/ppermute | solution.py:48
  138.5 5.9 %collective-permute-start.18 = (f32[3,1,512]{2,1,0:T(1,128)S(1)}, f32[3,1,512]{2,1,0:T(1,128)S(1)}, u32[]{:S(2)}, u32[]{:S(2)}) collective-permute-start(f32[3,1,512]{2,1,0:T(1,128)S(1)} %get-tuple-element.63), channel_id=1, source_target_pairs={{1,0},{2,1},{3,2},{4,3},{5,4},{6,5},{7,6},{9,8},{10,9},{11,10},{12... | collective-permute-start | bytes 18440 | tf_op jit(solution)/shard_map/ppermute | solution.py:49
  140.5 6.4 %collective-permute-start.17 = (f32[3,1,512]{2,1,0:T(1,128)S(1)}, f32[3,1,512]{2,1,0:T(1,128)S(1)}, u32[]{:S(2)}, u32[]{:S(2)}) collective-permute-start(f32[3,1,512]{2,1,0:T(1,128)S(1)} %get-tuple-element.62), channel_id=1, source_target_pairs={{0,1},{1,2},{2,3},{3,4},{4,5},{5,6},{6,7},{8,9},{9,10},{10,11},{11... | collective-permute-start | bytes 18440 | tf_op jit(solution)/shard_map/ppermute | solution.py:48
Sparse Core Ops, SparseCore 0:
  32.0 65.1 all-gather.1
